TPU v7x, 32 devices: a whole 2x2x4 slice. The times are simulated.
32 devices in a mesh: row: 8 (over z, y), col: 4 (over x, core).
Axes of the slice: x: 2, y: 2, z: 4, core: 2. Of those that a mesh axis runs over, the one named last changes fastest.
Arguments:
- a11: float32 [256, 256], replicated, as said below
- linv11: float32 [256, 256], replicated, as said below
- a21: float32 [16384, 256], P(('row', 'col')), may hold values from -6 to 6
- l21: float32 [16384, 256], P(('row', 'col')), may hold values from -0.4 to 0.4
- a22: float32 [16384, 16384], P('row', 'col'), may hold values from -6 to 6
Outputs:
- diag_block: float32 [256, 256], replicated
- panel: float32 [16384, 256], P(('row', 'col'))
- trailing: float32 [16384, 16384], P('row', 'col')
Inputs may be any that keep to these rules, and one draw needn't show every extreme that they name: `a11`: symmetric. `linv11`: lower triangular with a positive diagonal.
All inputs are finite; a program needn't handle non-finite values.
Results may differ from a plain program's by a relative error of at most 0.00005.
Values sent between devices are 32-bit elements; how exact they have to be, the bound alone decides.
No kernel may reach another device: no remote copies, remote signals or barrier semaphores. Data moves between devices by JAX's collectives and lax.ppermute only.
A program may use at most 128 MiB of HBM per device.

v0:
```python
import jax
import jax.numpy as jnp
from jax import lax
from jax.sharding import PartitionSpec as P


def spread(value, axis, source):
    kept = jnp.where(lax.axis_index(axis) == source, value, 0).astype(value.dtype)
    return lax.psum(kept, axis)


def mult(a, b):
    return jnp.dot(a, b, precision=lax.Precision.HIGHEST, preferred_element_type=jnp.float32)


def body(a11, linv11, a21, l21, a22):
    width = a21.shape[1]
    diag_block = mult(mult(linv11, a11), linv11.T)
    correction = 0.5 * mult(l21, diag_block)
    half = mult(a21, linv11.T) - correction
    panel = half - correction
    packed = jnp.concatenate([half, l21], axis=1)
    n_row = lax.axis_size("row")
    n_col = lax.axis_size("col")
    groups = n_row // n_col
    mine = lax.all_gather(packed, "col", axis=0, tiled=True)
    col_index = lax.axis_index("col")
    parts = []
    for step in range(groups):
        parts.append(spread(mine, "row", col_index * groups + step))
    across = jnp.concatenate(parts, axis=0)
    flipped = jnp.concatenate([across[:, width:], across[:, :width]], axis=1)
    trailing = a22 - mult(mine, flipped.T)
    return (diag_block, panel, trailing)


def solution(mesh):
    return jax.shard_map(
        body,
        mesh=mesh,
        in_specs=(P(), P(), P(("row", "col"), None), P(("row", "col"), None), P("row", "col")),
        out_specs=(P(), P(("row", "col"), None), P("row", "col")),
        check_vma=False,
    )
```

profile of v0, /device:TPU:24, one launch (start us, length us, event | category | flops | bytes accessed | tf_op | source)
XLA Modules:
  0.0 400.9 jit_solution(4599625725168545182)
XLA Ops:
  7.2 0.0 copy-start
  7.2 0.0 all-gather.2.cloned.1.call-start
  7.2 1.5 fusion.7
  8.7 1.4 fusion.8
  10.1 0.0 copy-start.4
  10.1 1.3 copy.8
  11.4 2.1 fusion.3
  13.5 0.0 copy-done
  13.5 1.6 fusion.6
  15.2 1.0 pad_maximum_fusion
  16.2 0.0 all-gather.2.cloned.1.call-update
  16.2 0.0 all-reduce.3.cloned.1.call-start
  16.3 35.6 %all-gather.2.cloned.1.call-done = f32[2048,512]{0,1:T(8,128)} async-done(((f32[512,512]{0,1:T(8,128)}), f32[2048,512]{0,1:T(8,128)}) %all-gather.2.cloned.1.call-update) | async-done | bytes 4194320 | tf_op jit(solution)/shard_map/all_gather | solution.py:26
  51.8 6.9 %broadcast_select_fusion = (f32[2048,512]{0,1:T(8,128)}, f32[2048,512]{0,1:T(8,128)}) fusion(f32[2048,512]{0,1:T(8,128)} %all-gather.2.cloned.1.call-done, pred[]{:T(512)S(6)} %eq.7, pred[]{:T(512)S(6)} %eq.6), kind=kLoop, calls=%fused_computation.4 | loop fusion | flops 2097152 | bytes 12582914 | tf_op jit(solution)/shard_map/jit(_where)/select_n | solution.py:8
  58.7 0.0 copy-done.4
  58.7 0.0 all-reduce.3.cloned.1.call-update
  58.7 1.0 copy.9
  59.7 267.6 %all-reduce.3.cloned.1.call-done = (f32[2048,512]{0,1:T(8,128)}, f32[2048,512]{0,1:T(8,128)}) async-done(((f32[2048,512]{0,1:T(8,128)}, f32[2048,512]{0,1:T(8,128)}), (f32[2048,512]{0,1:T(8,128)}, f32[2048,512]{0,1:T(8,128)})) %all-reduce.3.cloned.1.call-update) | async-done | bytes 8388624 | tf_op jit(solution)/shard_map/psum | solution.py:9
  327.3 2.6 constant_dynamic-update-slice_fusion.1
  329.9 0.8 copy-done.3
  330.8 0.5 constant_dynamic-update-slice_fusion
  331.3 1.0 fusion.5
  332.3 1.2 copy-done.2
  333.4 60.6 %convolution_subtract_fusion = f32[2048,4096]{1,0:T(8,128)} fusion(f32[2048,4096]{1,0:T(8,128)} %param.9, f32[2048,512]{0,1:T(8,128)S(1)} %copy-done.2, f32[4096,256]{0,1:T(8,128)S(1)} %get-tuple-element.9, f32[4096,256]{0,1:T(8,128)S(1)} %get-tuple-element.8), kind=kOutput, calls=%fused_computation | convolution fusion | flops 51550093312 | bytes 79691776 | tf_op jit(solution)/shard_map/dot_general | solution.py:13
  (4 shorter events, 0.0 us)
Async XLA Ops:
  7.2 6.4 %copy-start = (f32[512,256]{1,0:T(8,128)S(1)}, f32[512,256]{1,0:T(8,128)}, u32[]{:S(2)}) copy-start(f32[512,256]{1,0:T(8,128)} %param.7) | copy-start | bytes 1572868
  7.2 44.6 %all-gather.2.cloned.1.call-start = ((), (), s32[]{:S(2)}) async-start(), calls=%async_computation | async-start | bytes 5242880 | tf_op jit(solution)/shard_map/all_gather | solution.py:26
  10.1 48.6 %copy-start.4 = (f32[256,256]{1,0:T(8,128)}, f32[256,256]{1,0:T(8,128)S(1)}, u32[]{:S(2)}) copy-start(f32[256,256]{1,0:T(8,128)S(1)} %fusion.8) | copy-start | bytes 786436
  16.2 311.1 %all-reduce.3.cloned.1.call-start = ((), (), s32[]{:S(2)}) async-start(), calls=%async_computation.1 | async-start | bytes 16777216 | tf_op jit(solution)/shard_map/psum | solution.py:9
  327.3 3.4 copy-start.3
  331.3 2.2 copy-start.2
  333.4 60.6 %copy-start.1 = (f32[512,256]{1,0:T(8,128)S(1)}, f32[512,256]{1,0:T(8,128)}, u32[]{:S(2)}) copy-start(f32[512,256]{1,0:T(8,128)} %param.7) | copy-start | bytes 1572868
Sparse Core Ops, SparseCore 0:
  16.3 35.4 all-gather.1
  58.8 268.4 all-reduce.2
where the time goes:
time: 406 us; the launch traced here: 401 us
  waiting for transfers between devices  303 us (75%)
  matrix products  67.1 us (17%)
  between operations  14.1 us (3%)
  local copies, waits for them, and re-layouts  8.44 us (2%)
  other arithmetic  7.91 us (2%)
    psum x1, waiting for transfers between devices, spread(): return lax.psum(kept, axis)  268 us
    dot_general x5, matrix products, mult(): jnp.dot(a, b, precision=lax.Precision.HIGHEST, preferred_element_type=jnp...  67.1 us
    all_gather x1, waiting for transfers between devices, body(): mine = lax.all_gather(packed, 'col', axis=0, tiled=True)  35.6 us
  transfers between devices with their start and end apart: 2, of which 2 were waited for; matrix products, arithmetic and copies ran while one was open for 0% of the time, Pallas kernels for 0%

commit v1 on v0

v1 whole, which is shorter than its diff:
```python
import functools

import jax
import jax.numpy as jnp
from jax import lax
from jax.experimental import pallas as pl
from jax.experimental.pallas import tpu as pltpu
from jax.sharding import PartitionSpec as P

AXES = ("row", "col")
MIB = 1 << 20
LAG = 1
KLAG = 0


def mult(a, b):
    return jnp.dot(a, b, precision=lax.Precision.HIGHEST, preferred_element_type=jnp.float32)


def dot_t(a, b, precision=None):
    return lax.dot_general(a, b, (((1,), (1,)), ((), ())), precision=precision, preferred_element_type=jnp.float32)


def split(x):
    hi = x.astype(jnp.bfloat16)
    lo = (x - hi.astype(jnp.float32)).astype(jnp.bfloat16)
    return hi, lo


def front_kernel(a11_ref, linv_ref, a21_ref, l21_ref, diag_ref, panel_ref, *piece_refs):
    high = lax.Precision.HIGHEST
    linv = linv_ref[...]
    width = linv.shape[0]
    diag = dot_t(mult(linv, a11_ref[...]), linv, high)
    diag_ref[...] = diag
    rows = piece_refs[0].shape[0]
    for q, piece in enumerate(piece_refs):
        low = l21_ref[pl.ds(q * rows, rows), :]
        correction = 0.5 * mult(low, diag)
        half = dot_t(a21_ref[pl.ds(q * rows, rows), :], linv, high) - correction
        panel_ref[pl.ds(q * rows, rows), :] = half - correction
        piece[:, :width] = low
        piece[:, width:] = half


def rows_kernel(parts, me_ref, *refs):
    pieces, (hi_ref, lo_ref) = refs[:-2], refs[-2:]
    rows, both = pieces[0].shape
    width = both // 2
    for p, piece in enumerate(pieces):
        i, q = divmod(p, parts)
        at = pl.multiple_of(((me_ref[0] ^ i) * parts + q) * rows, rows)
        for dst, src in ((0, width), (width, 0)):
            hi, lo = split(piece[:, src : src + width])
            hi_ref[pl.ds(at, rows), dst : dst + width] = hi
            lo_ref[pl.ds(at, rows), dst : dst + width] = lo


def update_kernel(step, n_piece, block, table_ref, hi_ref, lo_ref, *refs):
    pieces = refs[:n_piece]
    scratch = refs[len(refs) - 2 * n_piece :]
    old_ref, new_ref = refs[n_piece], refs[len(refs) - 2 * n_piece - 1]
    rows, both = pieces[0].shape

    @pl.when(table_ref[step, 0] != 0)
    def _():
        for k, piece in enumerate(pieces):
            hi, lo = split(piece[...])
            scratch[2 * k][...] = hi
            scratch[2 * k + 1][...] = lo

        def body(a_hi, a_lo, *tiles):
            for k in range(n_piece):
                b_hi, b_lo = scratch[2 * k][...], scratch[2 * k + 1][...]
                left, low = a_hi[...], a_lo[...]
                total = dot_t(left, b_hi) + (dot_t(left, b_lo) + dot_t(low, b_hi))
                tiles[n_piece + k][...] = tiles[k][...] - total

        tile = [
            pl.BlockSpec((block, rows), lambda i, k=k: (i, table_ref[step, 1 + k]))
            for k in range(n_piece)
        ]
        operand = pl.BlockSpec((block, both), lambda i: (i, 0))
        pltpu.emit_pipeline(
            body,
            grid=(old_ref.shape[0] // block,),
            in_specs=[operand, operand] + tile,
            out_specs=tile,
        )(hi_ref, lo_ref, *([old_ref] * n_piece), *([new_ref] * n_piece))


def update(step, table, a_hi, a_lo, pieces, old, new):
    rows, both = pieces[0].shape
    n = len(pieces)
    height, columns = old.shape
    block = min(512, height)
    whole = pl.BlockSpec(memory_space=pl.ANY)
    held = pl.BlockSpec(memory_space=pltpu.VMEM)
    first = new is None
    return pl.pallas_call(
        functools.partial(update_kernel, step, n, block),
        grid_spec=pltpu.PrefetchScalarGridSpec(
            num_scalar_prefetch=1,
            grid=(),
            in_specs=[whole, whole] + [held] * n + [whole] * (1 if first else 2),
            out_specs=whole,
            scratch_shapes=[pltpu.VMEM((rows, both), jnp.bfloat16)] * (2 * n),
        ),
        out_shape=jax.ShapeDtypeStruct(old.shape, old.dtype),
        input_output_aliases={} if first else {3 + n + 1: 0},
        compiler_params=pltpu.CompilerParams(vmem_limit_bytes=24 * MIB),
        cost_estimate=pl.CostEstimate(
            flops=6 * n * height * rows * both,
            bytes_accessed=8 * n * height * rows + 4 * height * both,
            transcendentals=0,
        ),
        name="update",
    )(table, a_hi, a_lo, *pieces, old, *([] if first else [new]))


def place_pieces(across, line, pieces):
    for k, piece in enumerate(pieces):
        at = line[1 + k] * piece.shape[0]
        kept = lax.dynamic_slice_in_dim(across, at, piece.shape[0], 0)
        across = lax.dynamic_update_slice_in_dim(across, jnp.where(line[0] != 0, piece, kept), at, 0)
    return across


def solution(mesh):
    n_row, n_col = mesh.shape["row"], mesh.shape["col"]
    groups = n_row // n_col
    chain = n_col

    def at(place, g, c):
        return (place * groups + g) * n_col + c

    everyone = [(place, g, c) for place in range(chain) for g in range(groups) for c in range(n_col)]

    def sign(c):
        return 1 if c < n_col // 2 else -1

    def ahead(place, c):
        return (place + sign(c)) % chain

    ring = [(at(p, g, c), at(ahead(p, c), g, c)) for p, g, c in everyone]

    def swap_group(bit):
        return [(at(p, g, c), at(p, g ^ bit, c)) for p, g, c in everyone]

    def swap_col(bit):
        return [(at(p, g, c), at(p, g, c ^ bit)) for p, g, c in everyone]

    def send(value, pairs):
        return lax.ppermute(value, AXES, pairs)

    def body(a11, linv11, a21, l21, a22):
        rows, width = l21.shape
        parts = 2 if rows % 256 == 0 else 1
        r, c = lax.axis_index("row"), lax.axis_index("col")
        place, g = r // groups, r % groups
        far = jnp.where(c < n_col // 2, place - c, c - place) % chain

        piece = jax.ShapeDtypeStruct((rows // parts, 2 * width), jnp.float32)
        diag_block, panel, *own = pl.pallas_call(
            front_kernel,
            out_shape=[
                jax.ShapeDtypeStruct(a11.shape, jnp.float32),
                jax.ShapeDtypeStruct(a21.shape, jnp.float32),
            ]
            + [piece] * parts,
            compiler_params=pltpu.CompilerParams(vmem_limit_bytes=24 * MIB),
            name="front",
        )(a11, linv11, a21, l21)

        held = {0: own}
        bit = n_col // 2
        while bit:
            for i in sorted(held):
                held[i | bit] = [send(v, swap_col(bit)) for v in held[i]]
            bit //= 2
        source = [v for i in range(n_col) for v in held[i]]

        wide = rows // parts % 128 == 0
        a_hi, a_lo = pl.pallas_call(
            functools.partial(rows_kernel, parts),
            in_specs=[pl.BlockSpec(memory_space=pltpu.SMEM)] + [pl.BlockSpec(memory_space=pltpu.VMEM)] * len(source),
            out_shape=[jax.ShapeDtypeStruct((n_col * rows, 2 * width), jnp.bfloat16)] * 2,
            compiler_params=pltpu.CompilerParams(vmem_limit_bytes=32 * MIB),
            name="rows",
        )(c.astype(jnp.int32)[None], *source)

        count = len(source)
        steps = count + chain - 1
        index = jnp.arange(steps, dtype=jnp.int32) - far
        good = (index >= 0) & (index < count)
        index = jnp.clip(index, 0, count - 1)
        column = (c ^ (index // parts)) * parts + index % parts
        table = jnp.stack(
            [good.astype(jnp.int32)] + [(g ^ other) * n_col * parts + column for other in range(groups)], axis=1
        ).astype(jnp.int32)

        trailing = None
        across = jnp.zeros((a22.shape[1], 2 * width), jnp.float32)
        current = source[0]
        others = []
        states = []
        for t in range(steps):
            others.append([send(current, swap_group(b)) for b in range(1, groups)])
            if wide:
                trailing = update(t, table, a_hi, a_lo, [current] + others[t], a22, trailing)
            else:
                across = place_pieces(across, table[t], [current] + others[t])
            states.append(trailing)
            if t + 1 < steps:
                following = send(current, ring)
                if t >= LAG:
                    following, others[t - LAG] = lax.optimization_barrier((following, others[t - LAG]))
                current = jnp.where(far == 0, source[t + 1], following) if t + 1 < count else following
        if not wide:
            left = a_hi.astype(jnp.float32) + a_lo.astype(jnp.float32)
            trailing = a22 - dot_t(left, across, lax.Precision.HIGHEST)
        return diag_block, panel, trailing

    return jax.shard_map(
        body,
        mesh=mesh,
        in_specs=(P(), P(), P(AXES, None), P(AXES, None), P("row", "col")),
        out_specs=(P(), P(AXES, None), P("row", "col")),
        check_vma=False,
    )
```

time: 406 us -> 195 us (0.48)
  waiting for transfers between devices: 303 us -> 51.8 us
  Pallas kernels: 0 us -> 72.4 us
  matrix products: 67.1 us -> 0 us
  starting transfers between devices: 0.08 us -> 57 us
  between operations: 14.1 us -> 0.79 us
  other arithmetic: 7.91 us -> 1.65 us
    psum x1 -> x0, waiting for transfers between devices: 268 us -> none  [spread(): return lax.psum(kept, axis)]
    pallas_call x0 -> x13, Pallas kernels: none -> 72.4 us  [the longest x11 67.5 us: update(): pl.pallas_call(functools.partial(update_kernel, step, n, block), grid_spe...]
    dot_general x5 -> x0, matrix products: 67.1 us -> none  [mult(): jnp.dot(a, b, precision=lax.Precision.HIGHEST, preferred_element_type=jnp...]
    ppermute x0 -> x27, starting transfers between devices: none -> 57 us  [send(): return lax.ppermute(value, AXES, pairs)]
    ppermute x0 -> x27, waiting for transfers between devices: none -> 51.8 us  [send(): return lax.ppermute(value, AXES, pairs)]
    all_gather x1 -> x0, waiting for transfers between devices: 35.6 us -> none  [body(): mine = lax.all_gather(packed, 'col', axis=0, tiled=True)]
    select_n x1 -> x7, other arithmetic: 6.87 us -> 1.61 us  [body(): jnp.where(far == 0, source[t + 1], following)]
    unnamed x13 -> x36, local copies, waits for them, and re-layouts: 6.99 us -> 9.33 us
  transfers between devices with their start and end apart: 2 -> 27, of which waited for: 2 -> 10; matrix products, arithmetic and copies ran while one was open for 0% -> 1% of each run, Pallas kernels for 0% -> 32%
where the time goes in v1:
time: 195 us; the launch traced here: 193 us
  Pallas kernels  72.4 us (37%)
  starting transfers between devices  57 us (29%)
  waiting for transfers between devices  51.8 us (27%)
  local copies, waits for them, and re-layouts  9.42 us (5%)
    pallas_call x11, Pallas kernels, update(): pl.pallas_call(functools.partial(update_kernel, step, n, block), grid_spe...  67.5 us
    ppermute x27, starting transfers between devices, send(): return lax.ppermute(value, AXES, pairs)  57 us
    ppermute x27, waiting for transfers between devices, send(): return lax.ppermute(value, AXES, pairs)  51.8 us
    unnamed x36, local copies, waits for them, and re-layouts  9.33 us
  transfers between devices with their start and end apart: 27, of which 10 were waited for; matrix products, arithmetic and copies ran while one was open for 1% of the time, Pallas kernels for 32%

profile of v1, /device:TPU:24, one launch (start us, length us, event | category | flops | bytes accessed | tf_op | source)
XLA Modules:
  0.0 193.0 jit_solution(1930117739706887101)
XLA Ops:
  4.6 2.8 %front.1 = (f32[256,256]{1,0:T(8,128)}, f32[512,256]{1,0:T(8,128)}, f32[256,512]{1,0:T(8,128)S(1)}, f32[256,512]{1,0:T(8,128)S(1)}) custom-call(f32[256,256]{1,0:T(8,128)S(1)} %copy-done.16, f32[256,256]{1,0:T(8,128)S(1)} %copy-done.17, f32[512,256]{1,0:T(8,128)S(1)} %copy-done.14, f32[512,256]{1,0:T(8,128)S(1)} %copy-done.15), custom_call_target="tpu_custom_call" | custom-call | tf_op jit(solution)/shard_map/front/pallas_call | solution.py:164
  9.1 11.9 %collective-permute-done.6 = f32[256,512]{1,0:T(8,128)S(1)} collective-permute-done((f32[256,512]{1,0:T(8,128)S(1)}, f32[256,512]{1,0:T(8,128)S(1)}, u32[]{:S(2)}, u32[]{:S(2)}) %collective-permute-start.6) | collective-permute-done | bytes 524320 | tf_op jit(solution)/shard_map/ppermute | solution.py:154
  25.6 8.4 %collective-permute-done.7 = f32[256,512]{1,0:T(8,128)S(1)} collective-permute-done((f32[256,512]{1,0:T(8,128)S(1)}, f32[256,512]{1,0:T(8,128)S(1)}, u32[]{:S(2)}, u32[]{:S(2)}) %collective-permute-start.7) | collective-permute-done | bytes 524320 | tf_op jit(solution)/shard_map/ppermute | solution.py:154
  34.1 4.3 %collective-permute-start.9 = (f32[256,512]{1,0:T(8,128)S(1)}, f32[256,512]{1,0:T(8,128)S(1)}, u32[]{:S(2)}, u32[]{:S(2)}) collective-permute-start(f32[256,512]{1,0:T(8,128)S(1)} %broadcast_select_fusion.5.refs_0_), channel_id=1, source_target_pairs={{0,8},{1,9},{2,26},{3,27},{4,12},{5,13},{6,30},{7,31},{8,16},{9,17... | collective-permute-start | bytes 1572872 | tf_op jit(solution)/shard_map/ppermute | solution.py:154
  39.6 8.4 %collective-permute-done.9 = f32[256,512]{1,0:T(8,128)S(1)} collective-permute-done((f32[256,512]{1,0:T(8,128)S(1)}, f32[256,512]{1,0:T(8,128)S(1)}, u32[]{:S(2)}, u32[]{:S(2)}) %collective-permute-start.9) | collective-permute-done | bytes 524320 | tf_op jit(solution)/shard_map/ppermute | solution.py:154
  48.1 4.3 %collective-permute-start.11 = (f32[256,512]{1,0:T(8,128)S(1)}, f32[256,512]{1,0:T(8,128)S(1)}, u32[]{:S(2)}, u32[]{:S(2)}) collective-permute-start(f32[256,512]{1,0:T(8,128)S(1)} %broadcast_select_fusion.4.refs_0_), channel_id=1, source_target_pairs={{0,8},{1,9},{2,26},{3,27},{4,12},{5,13},{6,30},{7,31},{8,16},{9,17... | collective-permute-start | bytes 1572872 | tf_op jit(solution)/shard_map/ppermute | solution.py:154
  55.5 5.7 %collective-permute-done.11 = f32[256,512]{1,0:T(8,128)S(1)} collective-permute-done((f32[256,512]{1,0:T(8,128)S(1)}, f32[256,512]{1,0:T(8,128)S(1)}, u32[]{:S(2)}, u32[]{:S(2)}) %collective-permute-start.11) | collective-permute-done | bytes 524320 | tf_op jit(solution)/shard_map/ppermute | solution.py:154
  61.3 6.2 %collective-permute-done.2.refs_4_ = f32[256,512]{1,0:T(8,128)} collective-permute-done((f32[256,512]{1,0:T(8,128)S(1)}, f32[256,512]{1,0:T(8,128)}, u32[]{:S(2)}, u32[]{:S(2)}) %collective-permute-start.2) | collective-permute-done | bytes 524320 | tf_op jit(solution)/shard_map/ppermute | solution.py:154
  67.5 3.5 %collective-permute-start.13 = (f32[256,512]{1,0:T(8,128)S(1)}, f32[256,512]{1,0:T(8,128)S(1)}, u32[]{:S(2)}, u32[]{:S(2)}) collective-permute-start(f32[256,512]{1,0:T(8,128)S(1)} %broadcast_select_fusion.3.refs_0_), channel_id=1, source_target_pairs={{0,8},{1,9},{2,26},{3,27},{4,12},{5,13},{6,30},{7,31},{8,16},{9,17... | collective-permute-start | bytes 1572872 | tf_op jit(solution)/shard_map/ppermute | solution.py:154
  71.0 3.8 %collective-permute-done.3.refs_5_ = f32[256,512]{1,0:T(8,128)} collective-permute-done((f32[256,512]{1,0:T(8,128)S(1)}, f32[256,512]{1,0:T(8,128)}, u32[]{:S(2)}, u32[]{:S(2)}) %collective-permute-start.3) | collective-permute-done | bytes 524320 | tf_op jit(solution)/shard_map/ppermute | solution.py:154
  77.8 5.4 %collective-permute-start.15 = (f32[256,512]{1,0:T(8,128)S(1)}, f32[256,512]{1,0:T(8,128)}, u32[]{:S(2)}, u32[]{:S(2)}) collective-permute-start(f32[256,512]{1,0:T(8,128)S(1)} %broadcast_select_fusion.2.refs_0_), channel_id=1, source_target_pairs={{0,8},{1,9},{2,26},{3,27},{4,12},{5,13},{6,30},{7,31},{8,16},{9,17... | collective-permute-start | bytes 1572872 | tf_op jit(solution)/shard_map/ppermute | solution.py:154
  86.4 2.2 %rows.1 = (bf16[2048,512]{1,0:T(8,128)(2,1)S(1)}, bf16[2048,512]{1,0:T(8,128)(2,1)S(1)}) custom-call(s32[1]{0:T(128)} %bitcast.me_ref, f32[256,512]{1,0:T(8,128)S(1)} %get-tuple-element.20.refs_0_, f32[256,512]{1,0:T(8,128)S(1)} %copy-done.1, f32[256,512]{1,0:T(8,128)S(1)} %copy-done.3, f32[256,512]{1,0:T(8,128)S(1)} %copy-done.5, ...), custom_call_target="tpu_custom_call" | custom-call | tf_op jit(solution)/shard_map/rows/pallas_call | solution.py:184
  92.1 4.4 %collective-permute-start.17 = (f32[256,512]{1,0:T(8,128)S(1)}, f32[256,512]{1,0:T(8,128)S(1)}, u32[]{:S(2)}, u32[]{:S(2)}) collective-permute-start(f32[256,512]{1,0:T(8,128)S(1)} %broadcast_select_fusion.1.refs_0_), channel_id=1, source_target_pairs={{0,8},{1,9},{2,26},{3,27},{4,12},{5,13},{6,30},{7,31},{8,16},{9,17... | collective-permute-start | bytes 1572872 | tf_op jit(solution)/shard_map/ppermute | solution.py:154
  99.9 3.1 %collective-permute-done.18.refs_1_ = f32[256,512]{1,0:T(8,128)S(1)} collective-permute-done((f32[256,512]{1,0:T(8,128)S(1)}, f32[256,512]{1,0:T(8,128)S(1)}, u32[]{:S(2)}, u32[]{:S(2)}) %collective-permute-start.18) | collective-permute-done | bytes 524320 | tf_op jit(solution)/shard_map/ppermute | solution.py:154
  104.3 11.1 %collective-permute-start.19 = (f32[256,512]{1,0:T(8,128)S(1)}, f32[256,512]{1,0:T(8,128)S(1)}, u32[]{:S(2)}, u32[]{:S(2)}) collective-permute-start(f32[256,512]{1,0:T(8,128)S(1)} %broadcast_select_fusion.refs_0_), channel_id=1, source_target_pairs={{0,8},{1,9},{2,26},{3,27},{4,12},{5,13},{6,30},{7,31},{8,16},{9,17... | collective-permute-start | bytes 1572872 | tf_op jit(solution)/shard_map/ppermute | solution.py:154
  116.1 8.0 %update.14.refs_3_ = f32[2048,4096]{1,0:T(8,128)} custom-call(s32[11,3]{1,0:T(8,128)S(1)} %copy.28.table_ref, bf16[2048,512]{1,0:T(8,128)(2,1)S(1)} %get-tuple-element.22.hi_ref, bf16[2048,512]{1,0:T(8,128)(2,1)S(1)} %get-tuple-element.23.lo_ref, f32[256,512]{1,0:T(8,128)S(1)} %broadcast_select_fusion.4.refs_0_, ...), custom_call_target="tpu_custom_call", output_to_operand_aliasing={{}: (6, {})} | custom-call | flops 3221225472 | bytes 12582912 | tf_op jit(solution)/shard_map/update/pallas_call | solution.py:100
  125.7 7.4 %collective-permute-start.21 = (f32[256,512]{1,0:T(8,128)S(1)}, f32[256,512]{1,0:T(8,128)S(1)}, u32[]{:S(2)}, u32[]{:S(2)}) collective-permute-start(f32[256,512]{1,0:T(8,128)S(1)} %collective-permute-done.19.refs_0_), channel_id=1, source_target_pairs={{0,8},{1,9},{2,26},{3,27},{4,12},{5,13},{6,30},{7,31},{8,16},{9,17... | collective-permute-start | bytes 1572872 | tf_op jit(solution)/shard_map/ppermute | solution.py:154
  133.0 9.1 %update.15.refs_3_ = f32[2048,4096]{1,0:T(8,128)} custom-call(s32[11,3]{1,0:T(8,128)S(1)} %copy.28.table_ref, bf16[2048,512]{1,0:T(8,128)(2,1)S(1)} %get-tuple-element.22.hi_ref, bf16[2048,512]{1,0:T(8,128)(2,1)S(1)} %get-tuple-element.23.lo_ref, f32[256,512]{1,0:T(8,128)S(1)} %broadcast_select_fusion.3.refs_0_, ...), custom_call_target="tpu_custom_call", output_to_operand_aliasing={{}: (6, {})} | custom-call | flops 3221225472 | bytes 12582912 | tf_op jit(solution)/shard_map/update/pallas_call | solution.py:100
  142.1 8.2 %update.16.refs_3_ = f32[2048,4096]{1,0:T(8,128)} custom-call(s32[11,3]{1,0:T(8,128)S(1)} %copy.28.table_ref, bf16[2048,512]{1,0:T(8,128)(2,1)S(1)} %get-tuple-element.22.hi_ref, bf16[2048,512]{1,0:T(8,128)(2,1)S(1)} %get-tuple-element.23.lo_ref, f32[256,512]{1,0:T(8,128)S(1)} %broadcast_select_fusion.2.refs_0_, ...), custom_call_target="tpu_custom_call", output_to_operand_aliasing={{}: (6, {})} | custom-call | flops 3221225472 | bytes 12582912 | tf_op jit(solution)/shard_map/update/pallas_call | solution.py:100
  150.8 8.0 %update.17.refs_3_ = f32[2048,4096]{1,0:T(8,128)} custom-call(s32[11,3]{1,0:T(8,128)S(1)} %copy.28.table_ref, bf16[2048,512]{1,0:T(8,128)(2,1)S(1)} %get-tuple-element.22.hi_ref, bf16[2048,512]{1,0:T(8,128)(2,1)S(1)} %get-tuple-element.23.lo_ref, f32[256,512]{1,0:T(8,128)S(1)} %broadcast_select_fusion.1.refs_0_, ...), custom_call_target="tpu_custom_call", output_to_operand_aliasing={{}: (6, {})} | custom-call | flops 3221225472 | bytes 12582912 | tf_op jit(solution)/shard_map/update/pallas_call | solution.py:100
  160.4 8.0 %update.18.refs_3_ = f32[2048,4096]{1,0:T(8,128)} custom-call(s32[11,3]{1,0:T(8,128)S(1)} %copy.28.table_ref, bf16[2048,512]{1,0:T(8,128)(2,1)S(1)} %get-tuple-element.22.hi_ref, bf16[2048,512]{1,0:T(8,128)(2,1)S(1)} %get-tuple-element.23.lo_ref, f32[256,512]{1,0:T(8,128)S(1)} %broadcast_select_fusion.refs_0_, ...), custom_call_target="tpu_custom_call", output_to_operand_aliasing={{}: (6, {})} | custom-call | flops 3221225472 | bytes 12582912 | tf_op jit(solution)/shard_map/update/pallas_call | solution.py:100
  168.9 8.0 %update.19.refs_3_ = f32[2048,4096]{1,0:T(8,128)} custom-call(s32[11,3]{1,0:T(8,128)S(1)} %copy.28.table_ref, bf16[2048,512]{1,0:T(8,128)(2,1)S(1)} %get-tuple-element.22.hi_ref, bf16[2048,512]{1,0:T(8,128)(2,1)S(1)} %get-tuple-element.23.lo_ref, f32[256,512]{1,0:T(8,128)S(1)} %collective-permute-done.19.refs_0_, ...), custom_call_target="tpu_custom_call", output_to_operand_aliasing={{}: (6, {})} | custom-call | flops 3221225472 | bytes 12582912 | tf_op jit(solution)/shard_map/update/pallas_call | solution.py:100
  177.0 8.0 %update.20.refs_3_ = f32[2048,4096]{1,0:T(8,128)} custom-call(s32[11,3]{1,0:T(8,128)S(1)} %copy.28.table_ref, bf16[2048,512]{1,0:T(8,128)(2,1)S(1)} %get-tuple-element.22.hi_ref, bf16[2048,512]{1,0:T(8,128)(2,1)S(1)} %get-tuple-element.23.lo_ref, f32[256,512]{1,0:T(8,128)S(1)} %collective-permute-done.21.refs_0_, ...), custom_call_target="tpu_custom_call", output_to_operand_aliasing={{}: (6, {})} | custom-call | flops 3221225472 | bytes 12582912 | tf_op jit(solution)/shard_map/update/pallas_call | solution.py:100
  185.0 8.0 %update.21 = f32[2048,4096]{1,0:T(8,128)} custom-call(s32[11,3]{1,0:T(8,128)S(1)} %copy.28.table_ref, bf16[2048,512]{1,0:T(8,128)(2,1)S(1)} %get-tuple-element.22.hi_ref, bf16[2048,512]{1,0:T(8,128)(2,1)S(1)} %get-tuple-element.23.lo_ref, f32[256,512]{1,0:T(8,128)S(1)} %collective-permute-done.23.refs_0_, ...), custom_call_target="tpu_custom_call", output_to_operand_aliasing={{}: (6, {})} | custom-call | flops 3221225472 | bytes 12582912 | tf_op jit(solution)/shard_map/update/pallas_call | solution.py:100
  (90 shorter events, 34.0 us)
Async XLA Ops:
  7.4 13.7 %collective-permute-start.6 = (f32[256,512]{1,0:T(8,128)S(1)}, f32[256,512]{1,0:T(8,128)S(1)}, u32[]{:S(2)}, u32[]{:S(2)}) collective-permute-start(f32[256,512]{1,0:T(8,128)S(1)} %get-tuple-element.20.refs_0_), channel_id=1, source_target_pairs={{0,8},{1,9},{2,26},{3,27},{4,12},{5,13},{6,30},{7,31},{8,16},{9,17... | collective-permute-start | bytes 1572872 | tf_op jit(solution)/shard_map/ppermute | solution.py:154
  7.4 17.4 %collective-permute-start.8 = (f32[256,512]{1,0:T(8,128)S(1)}, f32[256,512]{1,0:T(8,128)S(1)}, u32[]{:S(2)}, u32[]{:S(2)}) collective-permute-start(f32[256,512]{1,0:T(8,128)S(1)} %get-tuple-element.20.refs_0_), channel_id=1, source_target_pairs={{0,4},{1,5},{2,6},{3,7},{4,0},{5,1},{6,2},{7,3},{8,12},{9,13},{10,... | collective-permute-start | bytes 1572872 | tf_op jit(solution)/shard_map/ppermute | solution.py:154
  21.1 12.8 %collective-permute-start.7 = (f32[256,512]{1,0:T(8,128)S(1)}, f32[256,512]{1,0:T(8,128)S(1)}, u32[]{:S(2)}, u32[]{:S(2)}) collective-permute-start(f32[256,512]{1,0:T(8,128)S(1)} %broadcast_select_fusion.6.refs_0_), channel_id=1, source_target_pairs={{0,8},{1,9},{2,26},{3,27},{4,12},{5,13},{6,30},{7,31},{8,16},{9,17... | collective-permute-start | bytes 1572872 | tf_op jit(solution)/shard_map/ppermute | solution.py:154
  23.3 10.7 %collective-permute-start = (f32[256,512]{1,0:T(8,128)S(1)}, f32[256,512]{1,0:T(8,128)S(1)}, u32[]{:S(2)}, u32[]{:S(2)}) collective-permute-start(f32[256,512]{1,0:T(8,128)S(1)} %get-tuple-element.20.refs_0_), channel_id=1, source_target_pairs={{0,1},{1,0},{2,3},{3,2},{4,5},{5,4},{6,7},{7,6},{8,9},{9,8},{10,11... | collective-permute-start | bytes 1572872 | tf_op jit(solution)/shard_map/ppermute | solution.py:154
  23.3 16.3 %collective-permute-start.10 = (f32[256,512]{1,0:T(8,128)S(1)}, f32[256,512]{1,0:T(8,128)S(1)}, u32[]{:S(2)}, u32[]{:S(2)}) collective-permute-start(f32[256,512]{1,0:T(8,128)S(1)} %broadcast_select_fusion.6.refs_0_), channel_id=1, source_target_pairs={{0,4},{1,5},{2,6},{3,7},{4,0},{5,1},{6,2},{7,3},{8,12},{9,13},{10,... | collective-permute-start | bytes 1572872 | tf_op jit(solution)/shard_map/ppermute | solution.py:154
  34.1 14.0 %collective-permute-start.9 = (f32[256,512]{1,0:T(8,128)S(1)}, f32[256,512]{1,0:T(8,128)S(1)}, u32[]{:S(2)}, u32[]{:S(2)}) collective-permute-start(f32[256,512]{1,0:T(8,128)S(1)} %broadcast_select_fusion.5.refs_0_), channel_id=1, source_target_pairs={{0,8},{1,9},{2,26},{3,27},{4,12},{5,13},{6,30},{7,31},{8,16},{9,17... | collective-permute-start | bytes 1572872 | tf_op jit(solution)/shard_map/ppermute | solution.py:154
  38.3 17.2 %collective-permute-start.12 = (f32[256,512]{1,0:T(8,128)S(1)}, f32[256,512]{1,0:T(8,128)S(1)}, u32[]{:S(2)}, u32[]{:S(2)}) collective-permute-start(f32[256,512]{1,0:T(8,128)S(1)} %broadcast_select_fusion.5.refs_0_), channel_id=1, source_target_pairs={{0,4},{1,5},{2,6},{3,7},{4,0},{5,1},{6,2},{7,3},{8,12},{9,13},{10,... | collective-permute-start | bytes 1572872 | tf_op jit(solution)/shard_map/ppermute | solution.py:154
  48.1 13.1 %collective-permute-start.11 = (f32[256,512]{1,0:T(8,128)S(1)}, f32[256,512]{1,0:T(8,128)S(1)}, u32[]{:S(2)}, u32[]{:S(2)}) collective-permute-start(f32[256,512]{1,0:T(8,128)S(1)} %broadcast_select_fusion.4.refs_0_), channel_id=1, source_target_pairs={{0,8},{1,9},{2,26},{3,27},{4,12},{5,13},{6,30},{7,31},{8,16},{9,17... | collective-permute-start | bytes 1572872 | tf_op jit(solution)/shard_map/ppermute | solution.py:154
  52.5 15.0 %collective-permute-start.2 = (f32[256,512]{1,0:T(8,128)S(1)}, f32[256,512]{1,0:T(8,128)}, u32[]{:S(2)}, u32[]{:S(2)}) collective-permute-start(f32[256,512]{1,0:T(8,128)S(1)} %get-tuple-element.20.refs_0_), channel_id=1, source_target_pairs={{0,2},{1,3},{2,0},{3,1},{4,6},{5,7},{6,4},{7,5},{8,10},{9,11},{10,... | collective-permute-start | bytes 1572872 | tf_op jit(solution)/shard_map/ppermute | solution.py:154
  53.1 21.7 %collective-permute-start.3 = (f32[256,512]{1,0:T(8,128)S(1)}, f32[256,512]{1,0:T(8,128)}, u32[]{:S(2)}, u32[]{:S(2)}) collective-permute-start(f32[256,512]{1,0:T(8,128)S(1)} %get-tuple-element.21.refs_1_), channel_id=1, source_target_pairs={{0,2},{1,3},{2,0},{3,1},{4,6},{5,7},{6,4},{7,5},{8,10},{9,11},{10,... | collective-permute-start | bytes 1572872 | tf_op jit(solution)/shard_map/ppermute | solution.py:154
  54.5 21.1 %collective-permute-start.14 = (f32[256,512]{1,0:T(8,128)S(1)}, f32[256,512]{1,0:T(8,128)S(1)}, u32[]{:S(2)}, u32[]{:S(2)}) collective-permute-start(f32[256,512]{1,0:T(8,128)S(1)} %broadcast_select_fusion.4.refs_0_), channel_id=1, source_target_pairs={{0,4},{1,5},{2,6},{3,7},{4,0},{5,1},{6,2},{7,3},{8,12},{9,13},{10,... | collective-permute-start | bytes 1572872 | tf_op jit(solution)/shard_map/ppermute | solution.py:154
  71.0 12.3 %collective-permute-start.4 = (f32[256,512]{1,0:T(8,128)}, f32[256,512]{1,0:T(8,128)}, u32[]{:S(2)}, u32[]{:S(2)}) collective-permute-start(f32[256,512]{1,0:T(8,128)} %collective-permute-done.2.refs_4_), channel_id=1, source_target_pairs={{0,1},{1,0},{2,3},{3,2},{4,5},{5,4},{6,7},{7,6},{8,9},{9,8},{10,11... | collective-permute-start | bytes 1572872 | tf_op jit(solution)/shard_map/ppermute | solution.py:154
  74.8 15.4 %collective-permute-start.16 = (f32[256,512]{1,0:T(8,128)S(1)}, f32[256,512]{1,0:T(8,128)}, u32[]{:S(2)}, u32[]{:S(2)}) collective-permute-start(f32[256,512]{1,0:T(8,128)S(1)} %broadcast_select_fusion.3.refs_0_), channel_id=1, source_target_pairs={{0,4},{1,5},{2,6},{3,7},{4,0},{5,1},{6,2},{7,3},{8,12},{9,13},{10,... | collective-permute-start | bytes 1572872 | tf_op jit(solution)/shard_map/ppermute | solution.py:154
  77.8 13.2 %collective-permute-start.15 = (f32[256,512]{1,0:T(8,128)S(1)}, f32[256,512]{1,0:T(8,128)}, u32[]{:S(2)}, u32[]{:S(2)}) collective-permute-start(f32[256,512]{1,0:T(8,128)S(1)} %broadcast_select_fusion.2.refs_0_), channel_id=1, source_target_pairs={{0,8},{1,9},{2,26},{3,27},{4,12},{5,13},{6,30},{7,31},{8,16},{9,17... | collective-permute-start | bytes 1572872 | tf_op jit(solution)/shard_map/ppermute | solution.py:154
  88.6 14.4 %collective-permute-start.18 = (f32[256,512]{1,0:T(8,128)S(1)}, f32[256,512]{1,0:T(8,128)S(1)}, u32[]{:S(2)}, u32[]{:S(2)}) collective-permute-start(f32[256,512]{1,0:T(8,128)S(1)} %broadcast_select_fusion.2.refs_0_), channel_id=1, source_target_pairs={{0,4},{1,5},{2,6},{3,7},{4,0},{5,1},{6,2},{7,3},{8,12},{9,13},{10,... | collective-permute-start | bytes 1572872 | tf_op jit(solution)/shard_map/ppermute | solution.py:154
  92.1 12.1 %collective-permute-start.17 = (f32[256,512]{1,0:T(8,128)S(1)}, f32[256,512]{1,0:T(8,128)S(1)}, u32[]{:S(2)}, u32[]{:S(2)}) collective-permute-start(f32[256,512]{1,0:T(8,128)S(1)} %broadcast_select_fusion.1.refs_0_), channel_id=1, source_target_pairs={{0,8},{1,9},{2,26},{3,27},{4,12},{5,13},{6,30},{7,31},{8,16},{9,17... | collective-permute-start | bytes 1572872 | tf_op jit(solution)/shard_map/ppermute | solution.py:154
  99.3 26.3 %collective-permute-start.20 = (f32[256,512]{1,0:T(8,128)S(1)}, f32[256,512]{1,0:T(8,128)S(1)}, u32[]{:S(2)}, u32[]{:S(2)}) collective-permute-start(f32[256,512]{1,0:T(8,128)S(1)} %broadcast_select_fusion.1.refs_0_), channel_id=1, source_target_pairs={{0,4},{1,5},{2,6},{3,7},{4,0},{5,1},{6,2},{7,3},{8,12},{9,13},{10,... | collective-permute-start | bytes 1572872 | tf_op jit(solution)/shard_map/ppermute | solution.py:154
  104.3 21.3 %collective-permute-start.19 = (f32[256,512]{1,0:T(8,128)S(1)}, f32[256,512]{1,0:T(8,128)S(1)}, u32[]{:S(2)}, u32[]{:S(2)}) collective-permute-start(f32[256,512]{1,0:T(8,128)S(1)} %broadcast_select_fusion.refs_0_), channel_id=1, source_target_pairs={{0,8},{1,9},{2,26},{3,27},{4,12},{5,13},{6,30},{7,31},{8,16},{9,17... | collective-permute-start | bytes 1572872 | tf_op jit(solution)/shard_map/ppermute | solution.py:154
  124.2 26.7 %collective-permute-start.22 = (f32[256,512]{1,0:T(8,128)S(1)}, f32[256,512]{1,0:T(8,128)S(1)}, u32[]{:S(2)}, u32[]{:S(2)}) collective-permute-start(f32[256,512]{1,0:T(8,128)S(1)} %broadcast_select_fusion.refs_0_), channel_id=1, source_target_pairs={{0,4},{1,5},{2,6},{3,7},{4,0},{5,1},{6,2},{7,3},{8,12},{9,13},{10,... | collective-permute-start | bytes 1572872 | tf_op jit(solution)/shard_map/ppermute | solution.py:154
  125.7 25.2 %collective-permute-start.21 = (f32[256,512]{1,0:T(8,128)S(1)}, f32[256,512]{1,0:T(8,128)S(1)}, u32[]{:S(2)}, u32[]{:S(2)}) collective-permute-start(f32[256,512]{1,0:T(8,128)S(1)} %collective-permute-done.19.refs_0_), channel_id=1, source_target_pairs={{0,8},{1,9},{2,26},{3,27},{4,12},{5,13},{6,30},{7,31},{8,16},{9,17... | collective-permute-start | bytes 1572872 | tf_op jit(solution)/shard_map/ppermute | solution.py:154
  150.3 18.1 %collective-permute-start.24 = (f32[256,512]{1,0:T(8,128)S(1)}, f32[256,512]{1,0:T(8,128)S(1)}, u32[]{:S(2)}, u32[]{:S(2)}) collective-permute-start(f32[256,512]{1,0:T(8,128)S(1)} %collective-permute-done.19.refs_0_), channel_id=1, source_target_pairs={{0,4},{1,5},{2,6},{3,7},{4,0},{5,1},{6,2},{7,3},{8,12},{9,13},{10,... | collective-permute-start | bytes 1572872 | tf_op jit(solution)/shard_map/ppermute | solution.py:154
  150.8 17.6 %collective-permute-start.23 = (f32[256,512]{1,0:T(8,128)S(1)}, f32[256,512]{1,0:T(8,128)S(1)}, u32[]{:S(2)}, u32[]{:S(2)}) collective-permute-start(f32[256,512]{1,0:T(8,128)S(1)} %collective-permute-done.21.refs_0_), channel_id=1, source_target_pairs={{0,8},{1,9},{2,26},{3,27},{4,12},{5,13},{6,30},{7,31},{8,16},{9,17... | collective-permute-start | bytes 1572872 | tf_op jit(solution)/shard_map/ppermute | solution.py:154
  158.9 18.1 %collective-permute-start.26 = (f32[256,512]{1,0:T(8,128)S(1)}, f32[256,512]{1,0:T(8,128)S(1)}, u32[]{:S(2)}, u32[]{:S(2)}) collective-permute-start(f32[256,512]{1,0:T(8,128)S(1)} %collective-permute-done.21.refs_0_), channel_id=1, source_target_pairs={{0,4},{1,5},{2,6},{3,7},{4,0},{5,1},{6,2},{7,3},{8,12},{9,13},{10,... | collective-permute-start | bytes 1572872 | tf_op jit(solution)/shard_map/ppermute | solution.py:154
  168.4 16.6 %collective-permute-start.25 = (f32[256,512]{1,0:T(8,128)S(1)}, f32[256,512]{1,0:T(8,128)S(1)}, u32[]{:S(2)}, u32[]{:S(2)}) collective-permute-start(f32[256,512]{1,0:T(8,128)S(1)} %collective-permute-done.23.refs_0_), channel_id=1, source_target_pairs={{0,4},{1,5},{2,6},{3,7},{4,0},{5,1},{6,2},{7,3},{8,12},{9,13},{10,... | collective-permute-start | bytes 1572872 | tf_op jit(solution)/shard_map/ppermute | solution.py:154
  (21 other events, 224.9 us)
